TPU v7x, 32 devices: a whole 2x2x4 slice. The times are simulated.
32 devices in a mesh: groups: 2 (over y), expert: 16 (over z, x, core), sub: 1.
Axes of the slice: x: 2, y: 2, z: 4, core: 2. Of those that a mesh axis runs over, the one named last changes fastest.
Arguments:
- gate_up: bfloat16 [512, 8, 2, 1024], P(('groups', 'expert', 'sub')), parts along dimension 0, may hold values from -8 to 8
- routes: int32 [512, 8], P(('groups', 'expert', 'sub')), parts along dimension 0, may hold values from 0 to 15, all different within a row; in each aligned block of 16 rows (0 to 15, 16 to 31, ...) at most 16 rows name the same one
Outputs:
- gram: float32 [32, 1024, 1024], P(('groups', 'expert'), 'sub'), parts along dimension 0
There are 2 independent parts, one for each index of `groups`. A program takes and returns all parts, laid end to end along the dimension named above; each array names one. Nothing has to cross between parts.
Inputs may be any that keep to these rules, and one draw needn't show every extreme that they name: `routes`: each token names 8 different experts; among the tokens of one device no expert is named more than 16 times, a bound that some block reaches; every expert is named somewhere.
All inputs are finite; a program needn't handle non-finite values.
Results may differ from a plain program's by a relative error of at most 0.0038.
Values may be sent and summed in bfloat16 or wider, within the bound.
A program may use at most 64 MiB of HBM per device.

v0:
```python
import jax
import jax.numpy as jnp
from jax import lax
from jax.sharding import PartitionSpec as P


def hidden_rows(rows, width):
    gate = rows[:, :width].astype(jnp.float32)
    upper = rows[:, width:].astype(jnp.float32)
    return (jax.nn.silu(gate) * upper).astype(jnp.bfloat16)


def per_device(gate_up, routes):
    tok_rows = gate_up.shape[0]
    picks = gate_up.shape[1]
    width = gate_up.shape[3]
    owners = lax.axis_size("expert")
    halves = lax.axis_size("sub")
    capacity = max(2, min(tok_rows, 2 * tok_rows * picks // owners))
    scale = 1.0 / (tok_rows * picks * halves)
    flat_routes = routes.reshape(-1)
    onehot = (flat_routes[:, None] == jnp.arange(owners, dtype=jnp.int32)[None, :]).astype(
        jnp.int32
    )
    ranks = jnp.sum(jnp.cumsum(onehot, axis=0) * onehot, axis=1) - 1
    slots = flat_routes * capacity + ranks
    payload = gate_up.reshape(tok_rows * picks, 2 * width)
    columns = payload.shape[1]
    send = jnp.zeros((owners * capacity, columns), jnp.bfloat16).at[slots].set(payload)
    send = send.reshape(owners, capacity, columns)
    received = lax.all_to_all(send, "expert", split_axis=0, concat_axis=0, tiled=True)
    rows_all = received.reshape(owners * capacity, columns)
    hidden = hidden_rows(rows_all, width)
    summed = lax.psum_scatter(
        jnp.einsum("rc,rd->cd", hidden, hidden, preferred_element_type=jnp.float32),
        "sub",
        scatter_dimension=0,
        tiled=True,
    )
    return (summed * scale)[None]


def solution(mesh):
    placed = (
        P(("groups", "expert", "sub"), None, None, None),
        P(("groups", "expert", "sub"), None),
    )
    return jax.shard_map(
        per_device,
        mesh=mesh,
        in_specs=placed,
        out_specs=P(("groups", "expert"), "sub", None),
        check_vma=False,
    )
```

profile of v0, /device:TPU:9, one launch (start us, length us, event | category | flops | bytes accessed | tf_op | source)
XLA Modules:
  0.0 40.0 jit_solution(5243324755329643662)
XLA Ops:
  0.0 0.7 %broadcast_multiply_fusion = s32[16,8]{0,1:T(8,128)S(1)} fusion(s32[16,8]{0,1:T(8,128)} %param.3), kind=kLoop, calls=%fused_computation.18 | loop fusion | flops 128 | bytes 1024 | tf_op jit(solution)/shard_map/mul | solution.py:26
  0.7 0.8 %copy.6 = s32[16,8]{1,0:T(8,128)S(1)} copy(s32[16,8]{0,1:T(8,128)} %param.3) | data formatting | bytes 1024 | tf_op args[1]
  1.4 0.1 copy.5
  1.5 0.1 mul.34
  1.6 0.1 eq.15
  1.7 0.1 fusion.11
  1.8 0.2 reduce_window_sum.11
  2.0 0.2 select_reduce_fusion
  2.1 1.2 %copy.7 = bf16[16,8,2,1024]{3,1,2,0:T(8,128)(2,1)S(1)} copy(bf16[16,8,2,1024]{3,2,1,0:T(2,128)(2,1)} %param.2) | data formatting | bytes 1048576
  3.3 1.7 %scatter_custom_fusion = bf16[256,2048]{1,0:T(8,128)(2,1)S(1)} fusion(s32[128]{0:T(128)S(1)} %fusion.12, bf16[128,2048]{1,0:T(8,128)(2,1)S(1)} %bitcast.16, bf16[]{:T(256)} %constant.7.clone.1), kind=kCustom, calls=%fused_computation.12 | custom fusion | bytes 1048578 | tf_op jit(solution)/shard_map/scatter | solution.py:29
  5.0 31.8 %all_to_all.5 = bf16[16,16,2048]{2,1,0:T(8,128)(2,1)S(1)} all-to-all(bf16[16,16,2048]{2,1,0:T(8,128)(2,1)S(1)} %bitcast.14), channel_id=1, replica_groups=mesh['groups'=2,'expert'=16,'sub'=1] {'expert'}, dimensions={0} | all-to-all | bytes 2097152 | tf_op jit(solution)/shard_map/all_to_all | solution.py:31
  36.8 3.2 %multiply_bitcast_fusion = f32[1,1024,1024]{2,1,0:T(8,128)} fusion(bf16[256,2048]{1,0:T(8,128)(2,1)S(1)} %bitcast.15), kind=kOutput, calls=%fused_computation.1 | convolution fusion | flops 540016640 | bytes 5242880 | tf_op jit(solution)/shard_map/rc,rd->cd/dot_general | solution.py:35
  (1 shorter events, 0.0 us)
where the time goes:
time: 40.8 us; the launch traced here: 40 us
  blocking collectives  31.8 us (78%)
  local copies, waits for them, and re-layouts  3.87 us (9%)
  matrix products  3.22 us (8%)
  other arithmetic  1.13 us (3%)
    all_to_all x1, blocking collectives, per_device(): lax.all_to_all(send, 'expert', split_axis=0, concat_axis=0, tiled=True)  31.8 us
    dot_general x1, matrix products, per_device(): jnp.einsum('rc,rd->cd', hidden, hidden, preferred_element_type=jnp.float32)  3.22 us
    unnamed x2, local copies, waits for them, and re-layouts  1.92 us
    scatter x1, local copies, waits for them, and re-layouts, per_device(): jnp.zeros((owners * capacity, columns), jnp.bfloat16).at[slots].set(payload)  1.71 us

commit v1 on v0

v1 whole, which is shorter than its diff:
```python
import functools

import jax
import jax.numpy as jnp
from jax import lax
from jax.experimental import pallas as pl
from jax.experimental.pallas import tpu as pltpu
from jax.sharding import PartitionSpec as P

MESH = pl.DeviceIdType.MESH


def hidden_rows(gate_up):
    gate = gate_up[..., 0, :].astype(jnp.float32)
    upper = gate_up[..., 1, :].astype(jnp.float32)
    return (jax.nn.silu(gate) * upper).astype(jnp.bfloat16)


def partner(me, owners, step):
    half = owners // 2
    mine, place = me // half, me % half
    far = (1 - mine) * half + (place + step) % half
    near = mine * half + (place + step + 1 - half) % half
    return jnp.where(step < half, far, near)


def exchange_kernel(owners, tok_rows, picks, hidden_ref, routes_ref, got_ref, send_ref, send_sem, recv_sem):
    me = lax.axis_index("expert")
    half = owners // 2
    mine, place = me // half, me % half

    def peer(step):
        if step < half:
            return (1 - mine) * half + (place + step) % half
        return mine * half + (place + step + 1 - half) % half

    barrier = pltpu.get_barrier_semaphore()
    for step in range(owners - 1):
        pl.semaphore_signal(barrier, inc=1, device_id={"expert": peer(step)}, device_id_type=MESH)

    entries = tok_rows * picks
    token = lax.broadcasted_iota(jnp.int32, (tok_rows, entries), 0)
    entry = lax.broadcasted_iota(jnp.int32, (tok_rows, entries), 1)
    spread = (entry // picks == token).astype(jnp.float32)
    by_pick = jnp.dot(routes_ref[...].astype(jnp.float32), spread, preferred_element_type=jnp.float32)
    pick = lax.broadcasted_iota(jnp.int32, (picks, entries), 0)
    entry = lax.broadcasted_iota(jnp.int32, (picks, entries), 1)
    flat = jnp.sum(jnp.where(entry % picks == pick, by_pick, 0.0), axis=0, keepdims=True).astype(jnp.int32)

    rows = owners * tok_rows
    row = lax.broadcasted_iota(jnp.int32, (rows, entries), 0)
    entry = lax.broadcasted_iota(jnp.int32, (rows, entries), 1)
    named = partner(me, owners, row // tok_rows)
    choose = jnp.where((flat == named) & (entry // picks == row % tok_rows), 1.0, 0.0).astype(jnp.bfloat16)
    placed = jnp.dot(choose, hidden_ref[...], preferred_element_type=jnp.float32).astype(jnp.bfloat16)
    last = rows - tok_rows
    send_ref[...] = placed[:last]
    got_ref[last:, :] = placed[last:]

    pl.semaphore_wait(barrier, owners - 1)
    copies = []
    for step in range(owners - 1):
        block = pl.ds(step * tok_rows, tok_rows)
        copy = pltpu.make_async_remote_copy(
            src_ref=send_ref.at[block],
            dst_ref=got_ref.at[block],
            send_sem=send_sem.at[step],
            recv_sem=recv_sem.at[step],
            device_id={"expert": peer(step)},
            device_id_type=MESH,
        )
        copy.start()
        copies.append(copy)
    for copy in copies:
        copy.wait()


def exchange(hidden, routes, owners):
    entries, width = hidden.shape
    picks, tok_rows = routes.shape
    rows = owners * tok_rows
    return pl.pallas_call(
        functools.partial(exchange_kernel, owners, tok_rows, picks),
        out_shape=jax.ShapeDtypeStruct((rows, width), jnp.bfloat16),
        in_specs=[pl.BlockSpec(memory_space=pltpu.VMEM)] * 2,
        out_specs=pl.BlockSpec(memory_space=pltpu.VMEM),
        scratch_shapes=[
            pltpu.VMEM((rows - tok_rows, width), jnp.bfloat16),
            pltpu.SemaphoreType.DMA((owners - 1,)),
            pltpu.SemaphoreType.DMA((owners - 1,)),
        ],
        compiler_params=pltpu.CompilerParams(
            collective_id=0, has_side_effects=True, vmem_limit_bytes=16 * 1024 * 1024
        ),
    )(hidden, routes)


def exchange_plain(hidden, routes, owners, capacity):
    entries, width = hidden.shape
    flat = routes.reshape(-1)
    onehot = (flat[:, None] == jnp.arange(owners, dtype=jnp.int32)[None, :]).astype(jnp.int32)
    ranks = jnp.sum(jnp.cumsum(onehot, axis=0) * onehot, axis=1) - 1
    slots = flat * capacity + ranks
    choose = (jnp.arange(owners * capacity, dtype=jnp.int32)[:, None] == slots[None, :]).astype(jnp.bfloat16)
    send = jnp.dot(choose, hidden, preferred_element_type=jnp.float32).astype(jnp.bfloat16)
    send = send.reshape(owners, capacity, width)
    return lax.all_to_all(send, "expert", split_axis=0, concat_axis=0, tiled=True).reshape(owners * capacity, width)


def per_device(gate_up, routes):
    tok_rows, picks, _, width = gate_up.shape
    owners = lax.axis_size("expert")
    halves = lax.axis_size("sub")
    capacity = max(2, min(tok_rows, 2 * tok_rows * picks // owners))
    scale = 1.0 / (tok_rows * picks * halves)
    hidden = hidden_rows(gate_up).reshape(tok_rows * picks, width)
    if capacity == tok_rows and tok_rows % 16 == 0 and owners % 2 == 0 and owners <= 32 and halves == 1:
        rows = exchange(hidden, routes.T, owners)
        gram = jnp.einsum("rc,rd->cd", rows, rows, preferred_element_type=jnp.float32)
    else:
        rows = exchange_plain(hidden, routes, owners, capacity)
        gram = jnp.einsum("rc,rd->cd", rows, rows, preferred_element_type=jnp.float32)
        if halves > 1:
            gram = lax.psum_scatter(gram, "sub", scatter_dimension=0, tiled=True)
    return (gram * scale)[None]


def solution(mesh):
    placed = (
        P(("groups", "expert", "sub"), None, None, None),
        P(("groups", "expert", "sub"), None),
    )
    return jax.shard_map(
        per_device,
        mesh=mesh,
        in_specs=placed,
        out_specs=P(("groups", "expert"), "sub", None),
        check_vma=False,
    )
```

time: 40.8 us -> 25.1 us (0.62)
  the two profiles are of different devices: /device:TPU:9 before, /device:TPU:0 now
where the time goes in v1:
time: 25.1 us; the launch traced here: 25 us
  Pallas kernels  19 us (76%)
  local copies, waits for them, and re-layouts  2.94 us (12%)
  matrix products  2.76 us (11%)
    pallas_call x1, Pallas kernels, exchange(): pl.pallas_call(functools.partial(exchange_kernel, owners, tok_rows, picks...  19 us
    dot_general x1, matrix products, per_device(): jnp.einsum('rc,rd->cd', rows, rows, preferred_element_type=jnp.float32)  2.76 us
    slice x1, local copies, waits for them, and re-layouts, hidden_rows(): gate = gate_up[..., 0, :].astype(jnp.float32)  2.26 us
    unnamed x2, local copies, waits for them, and re-layouts  0.68 us

profile of v1, /device:TPU:0, one launch (start us, length us, event | category | flops | bytes accessed | tf_op | source)
XLA Modules:
  0.0 25.0 jit_solution(7284414133575605707)
XLA Ops:
  0.0 2.3 %fusion.5 = (bf16[16,8,1,1024]{3,2,1,0:T(2,128)(2,1)S(1)}, bf16[16,8,1,1024]{3,2,1,0:T(2,128)(2,1)S(1)}) fusion(bf16[16,8,2,1024]{3,2,1,0:T(2,128)(2,1)} %param.2), kind=kLoop, calls=%fused_computation.10 | loop fusion | bytes 1048576 | tf_op jit(solution)/shard_map/slice | solution.py:14
  2.3 0.2 fusion.4.hidden_ref
  2.5 0.0 copy-start
  2.5 0.7 %copy-done = s32[16,8]{0,1:T(8,128)S(1)} copy-done((s32[16,8]{0,1:T(8,128)S(1)}, s32[16,8]{0,1:T(8,128)}, u32[]{:S(2)}) %copy-start) | copy-done | bytes 536
  3.2 19.0 %shard_map.28 = bf16[256,1024]{1,0:T(8,128)(2,1)S(1)} custom-call(bf16[128,1024]{1,0:T(8,128)(2,1)S(1)} %fusion.4.hidden_ref, s32[8,16]{1,0:T(8,128)S(1)} %bitcast.15), custom_call_target="tpu_custom_call" | custom-call | tf_op jit(solution)/shard_map/pallas_call | solution.py:82
  22.2 2.8 %multiply_bitcast_fusion = f32[1,1024,1024]{2,1,0:T(8,128)} fusion(bf16[256,1024]{1,0:T(8,128)(2,1)S(1)} %shard_map.28), kind=kOutput, calls=%fused_computation | convolution fusion | flops 537919488 | bytes 4718592 | tf_op jit(solution)/shard_map/rc,rd->cd/dot_general | solution.py:119
Async XLA Ops:
  2.5 0.7 %copy-start = (s32[16,8]{0,1:T(8,128)S(1)}, s32[16,8]{0,1:T(8,128)}, u32[]{:S(2)}) copy-start(s32[16,8]{0,1:T(8,128)} %param.3) | copy-start | bytes 1540

commit v2 on v1

v2 whole, which is shorter than its diff:
```python
import functools

import jax
import jax.numpy as jnp
from jax import lax
from jax.experimental import pallas as pl
from jax.experimental.pallas import tpu as pltpu
from jax.sharding import PartitionSpec as P

MESH = pl.DeviceIdType.MESH


def hidden_rows(gate_up):
    gate = gate_up[..., 0, :].astype(jnp.float32)
    upper = gate_up[..., 1, :].astype(jnp.float32)
    return (jax.nn.silu(gate) * upper).astype(jnp.bfloat16)


def partner(me, owners, quarter, step):
    half = owners // 2
    mine, plane, place = me // half, me // quarter, me % quarter
    group, turn = step // quarter, step % quarter
    if isinstance(step, int):
        plane_to = [(1 - mine) * 2, (1 - mine) * 2 + 1, mine * 2 + 1 - plane % 2, plane][group]
    else:
        plane_to = jnp.where(group < 2, (1 - mine) * 2 + group, jnp.where(group == 2, mine * 2 + 1 - plane % 2, plane))
    return plane_to * quarter + (place + turn + group // 3) % quarter


def exchange_kernel(
    owners, gate_up_ref, routes_ref, got_ref, raw_ref, named_ref, hidden_ref, send_ref, in_sem, send_sem, recv_sem
):
    me = lax.axis_index("expert")
    entries, _, width = gate_up_ref.shape
    picks, tok_rows = routes_ref.shape
    quarter = owners // 4
    pieces = in_sem.shape[0] - 1

    barrier = pltpu.get_barrier_semaphore()
    for step in range(owners - 1):
        pl.semaphore_signal(
            barrier, inc=1, device_id={"expert": partner(me, owners, quarter, step)}, device_id_type=MESH
        )

    routes_in = pltpu.make_async_copy(routes_ref, named_ref, in_sem.at[pieces])
    routes_in.start()
    part = entries // pieces
    loads = []
    for piece in range(pieces):
        span = pl.ds(piece * part, part)
        loads.append(pltpu.make_async_copy(gate_up_ref.at[span], raw_ref.at[span], in_sem.at[piece]))
        loads[-1].start()

    routes_in.wait()
    token = lax.broadcasted_iota(jnp.int32, (tok_rows, entries), 0)
    entry = lax.broadcasted_iota(jnp.int32, (tok_rows, entries), 1)
    spread = (entry // picks == token).astype(jnp.float32)
    by_pick = jnp.dot(named_ref[...].astype(jnp.float32), spread, preferred_element_type=jnp.float32)
    pick = lax.broadcasted_iota(jnp.int32, (picks, entries), 0)
    entry = lax.broadcasted_iota(jnp.int32, (picks, entries), 1)
    flat = jnp.sum(jnp.where(entry % picks == pick, by_pick, 0.0), axis=0, keepdims=True).astype(jnp.int32)

    rows = owners * tok_rows
    row = lax.broadcasted_iota(jnp.int32, (rows, 1), 0)
    goes_to = partner(me, owners, quarter, row // tok_rows)
    entry = lax.broadcasted_iota(jnp.int32, (rows, entries), 1)
    choose = jnp.where((flat == goes_to) & (entry // picks == row % tok_rows), 1.0, 0.0).astype(jnp.bfloat16)

    for piece in range(pieces):
        loads[piece].wait()
        span = pl.ds(piece * part, part)
        both = raw_ref[span].reshape(part, 2 * width)
        gate = both[:, :width].astype(jnp.float32)
        upper = both[:, width:].astype(jnp.float32)
        hidden_ref[span] = (jax.nn.silu(gate) * upper).astype(jnp.bfloat16)

    def place(first, count):
        picked = choose[first : first + count]
        return jnp.dot(picked, hidden_ref[...], preferred_element_type=jnp.float32).astype(jnp.bfloat16)

    middle, last = rows // 2, rows - tok_rows
    send_ref[:middle] = place(0, middle)
    pl.semaphore_wait(barrier, owners - 1)
    parity = (me // quarter) % 2

    def exchanged(step, slot):
        return pltpu.make_async_remote_copy(
            src_ref=send_ref.at[pl.ds(step * tok_rows, tok_rows)],
            dst_ref=got_ref.at[pl.ds(pl.multiple_of(slot * tok_rows, tok_rows), tok_rows)],
            send_sem=send_sem.at[step],
            recv_sem=recv_sem.at[slot],
            device_id={"expert": partner(me, owners, quarter, step)},
            device_id_type=MESH,
        )

    def send(step):
        slot = parity * quarter + step % quarter if step < owners // 2 else step
        exchanged(step, slot).start()

    for step in range(owners // 2):
        send(step)
    rest = place(middle, middle)
    send_ref[middle:] = rest[: last - middle]
    got_ref[last:, :] = rest[last - middle :]
    for step in range(owners // 2, owners - 1):
        send(step)
    for step in range(owners - 1):
        exchanged(step, step).wait()


def exchange(gate_up, routes, owners):
    entries, _, width = gate_up.shape
    picks, tok_rows = routes.shape
    rows = owners * tok_rows
    pieces = 4
    return pl.pallas_call(
        functools.partial(exchange_kernel, owners),
        out_shape=jax.ShapeDtypeStruct((rows, width), jnp.bfloat16),
        in_specs=[pl.BlockSpec(memory_space=pltpu.HBM)] * 2,
        out_specs=pl.BlockSpec(memory_space=pltpu.VMEM),
        scratch_shapes=[
            pltpu.VMEM((entries, 2, width), jnp.bfloat16),
            pltpu.VMEM((picks, tok_rows), jnp.int32),
            pltpu.VMEM((entries, width), jnp.bfloat16),
            pltpu.VMEM((rows - tok_rows, width), jnp.bfloat16),
            pltpu.SemaphoreType.DMA((pieces + 1,)),
            pltpu.SemaphoreType.DMA((owners - 1,)),
            pltpu.SemaphoreType.DMA((owners - 1,)),
        ],
        compiler_params=pltpu.CompilerParams(
            collective_id=0, has_side_effects=True, vmem_limit_bytes=54400 * 1024
        ),
    )(gate_up, routes)


def gram_kernel(scale, tiles, rows_ref, gram_ref, tile_ref, out_sem):
    width = rows_ref.shape[1]
    height = width // tiles
    writes = []
    for tile in range(tiles):
        span = pl.ds(tile * height, height)
        product = lax.dot_general(
            rows_ref[:, span], rows_ref[...], (((0,), (0,)), ((), ())), preferred_element_type=jnp.float32
        )
        tile_ref[span] = product * scale
        writes.append(pltpu.make_async_copy(tile_ref.at[span], gram_ref.at[span], out_sem.at[tile]))
        writes[-1].start()
    for write in writes:
        write.wait()


def gram_of(rows, scale):
    width = rows.shape[1]
    tiles = 8 if width % 1024 == 0 else 1
    return pl.pallas_call(
        functools.partial(gram_kernel, scale, tiles),
        out_shape=jax.ShapeDtypeStruct((width, width), jnp.float32),
        in_specs=[pl.BlockSpec(memory_space=pltpu.VMEM)],
        out_specs=pl.BlockSpec(memory_space=pltpu.HBM),
        scratch_shapes=[pltpu.VMEM((width, width), jnp.float32), pltpu.SemaphoreType.DMA((tiles,))],
        compiler_params=pltpu.CompilerParams(vmem_limit_bytes=32 * 1024 * 1024),
    )(rows)


def exchange_plain(hidden, routes, owners, capacity):
    entries, width = hidden.shape
    flat = routes.reshape(-1)
    onehot = (flat[:, None] == jnp.arange(owners, dtype=jnp.int32)[None, :]).astype(jnp.int32)
    ranks = jnp.sum(jnp.cumsum(onehot, axis=0) * onehot, axis=1) - 1
    slots = flat * capacity + ranks
    choose = (jnp.arange(owners * capacity, dtype=jnp.int32)[:, None] == slots[None, :]).astype(jnp.bfloat16)
    send = jnp.dot(choose, hidden, preferred_element_type=jnp.float32).astype(jnp.bfloat16)
    send = send.reshape(owners, capacity, width)
    return lax.all_to_all(send, "expert", split_axis=0, concat_axis=0, tiled=True).reshape(owners * capacity, width)


def per_device(gate_up, routes):
    tok_rows, picks, _, width = gate_up.shape
    owners = lax.axis_size("expert")
    halves = lax.axis_size("sub")
    capacity = max(2, min(tok_rows, 2 * tok_rows * picks // owners))
    scale = 1.0 / (tok_rows * picks * halves)
    if capacity == tok_rows and tok_rows % 16 == 0 and owners % 4 == 0 and owners <= 32 and halves == 1:
        rows = exchange(gate_up.reshape(tok_rows * picks, 2, width), routes.T, owners)
        return gram_of(rows, scale)[None]
    hidden = hidden_rows(gate_up).reshape(tok_rows * picks, width)
    rows = exchange_plain(hidden, routes, owners, capacity)
    gram = jnp.einsum("rc,rd->cd", rows, rows, preferred_element_type=jnp.float32)
    gram = lax.psum_scatter(gram, "sub", scatter_dimension=0, tiled=True)
    return (gram * scale)[None]


def solution(mesh):
    placed = (
        P(("groups", "expert", "sub"), None, None, None),
        P(("groups", "expert", "sub"), None),
    )
    return jax.shard_map(
        per_device,
        mesh=mesh,
        in_specs=placed,
        out_specs=P(("groups", "expert"), "sub", None),
        check_vma=False,
    )
```

time: 25.1 us -> 19.9 us (0.79)
  the two profiles are of different devices: /device:TPU:0 before, /device:TPU:9 now
where the time goes in v2:
time: 19.9 us; the launch traced here: 19.7 us
  Pallas kernels  19.1 us (96%)
  local copies, waits for them, and re-layouts  0.69 us (3%)
    pallas_call x1, Pallas kernels, exchange(): pl.pallas_call(functools.partial(exchange_kernel, owners), out_shape=jax....  16.7 us
    pallas_call x1, Pallas kernels, gram_of(): pl.pallas_call(functools.partial(gram_kernel, scale, tiles), out_shape=ja...  2.35 us
    unnamed x2, local copies, waits for them, and re-layouts  0.69 us

profile of v2, /device:TPU:9, one launch (start us, length us, event | category | flops | bytes accessed | tf_op | source)
XLA Modules:
  0.0 19.7 jit_solution(765230202922644724)
XLA Ops:
  0.0 0.0 copy-start
  0.0 0.7 %copy-done = s32[16,8]{0,1:T(8,128)S(1)} copy-done((s32[16,8]{0,1:T(8,128)S(1)}, s32[16,8]{0,1:T(8,128)}, u32[]{:S(2)}) %copy-start) | copy-done | bytes 536
  0.7 16.7 %shard_map.28.rows_ref = bf16[256,1024]{1,0:T(8,128)(2,1)S(1)} custom-call(bf16[128,2,1024]{2,1,0:T(2,128)(2,1)} %bitcast.4, s32[8,16]{1,0:T(8,128)S(1)} %bitcast.3), custom_call_target="tpu_custom_call" | custom-call | tf_op jit(solution)/shard_map/pallas_call | solution.py:116
  17.4 2.4 %shard_map.29 = f32[1024,1024]{1,0:T(8,128)} custom-call(bf16[256,1024]{1,0:T(8,128)(2,1)S(1)} %shard_map.28.rows_ref), custom_call_target="tpu_custom_call" | custom-call | tf_op jit(solution)/shard_map/pallas_call | solution.py:155
Async XLA Ops:
  0.0 0.7 %copy-start = (s32[16,8]{0,1:T(8,128)S(1)}, s32[16,8]{0,1:T(8,128)}, u32[]{:S(2)}) copy-start(s32[16,8]{0,1:T(8,128)} %param.3) | copy-start | bytes 1540

commit v3 on v2

--- a/solution.py
+++ b/solution.py
@@ -128,9 +128,9 @@
             pltpu.SemaphoreType.DMA((owners - 1,)),
         ],
         compiler_params=pltpu.CompilerParams(
-            collective_id=0, has_side_effects=True, vmem_limit_bytes=54400 * 1024
+            collective_id=0, has_side_effects=True, vmem_limit_bytes=32 * 1024 * 1024
         ),
-    )(gate_up, routes)
+    )(pltpu.with_memory_space_constraint(gate_up, pltpu.HBM), pltpu.with_memory_space_constraint(routes, pltpu.HBM))
 
 
 def gram_kernel(scale, tiles, rows_ref, gram_ref, tile_ref, out_sem):

time: 19.9 us -> 19.2 us (0.965)
  local copies, waits for them, and re-layouts: 0.69 us -> 0 us
    unnamed x2 -> x0, local copies, waits for them, and re-layouts: 0.69 us -> none
where the time goes in v3:
time: 19.2 us; the launch traced here: 19.1 us
  Pallas kernels  19 us (99%)
    pallas_call x1, Pallas kernels, exchange(): pl.pallas_call(functools.partial(exchange_kernel, owners), out_shape=jax....  16.7 us
    pallas_call x1, Pallas kernels, gram_of(): pl.pallas_call(functools.partial(gram_kernel, scale, tiles), out_shape=ja...  2.35 us

profile of v3, /device:TPU:9, one launch (start us, length us, event | category | flops | bytes accessed | tf_op | source)
XLA Modules:
  0.0 19.1 jit_solution(12730107750848704440)
XLA Ops:
  0.0 16.7 %shard_map.28.rows_ref = bf16[256,1024]{1,0:T(8,128)(2,1)S(1)} custom-call(bf16[128,2,1024]{2,1,0:T(2,128)(2,1)} %bitcast.3, s32[8,16]{1,0:T(8,128)} %bitcast.4), custom_call_target="tpu_custom_call" | custom-call | tf_op jit(solution)/shard_map/pallas_call | solution.py:116
  16.7 2.3 %shard_map.29 = f32[1024,1024]{1,0:T(8,128)} custom-call(bf16[256,1024]{1,0:T(8,128)(2,1)S(1)} %shard_map.28.rows_ref), custom_call_target="tpu_custom_call" | custom-call | tf_op jit(solution)/shard_map/pallas_call | solution.py:155

commit v4 on v3

--- a/solution.py
+++ b/solution.py
@@ -37,10 +37,21 @@
     pieces = in_sem.shape[0] - 1
 
     barrier = pltpu.get_barrier_semaphore()
-    for step in range(owners - 1):
-        pl.semaphore_signal(
-            barrier, inc=1, device_id={"expert": partner(me, owners, quarter, step)}, device_id_type=MESH
-        )
+    early = owners - quarter
+    plane, place_in = me // quarter, me % quarter
+
+    def greet(other):
+        pl.semaphore_signal(barrier, inc=1, device_id={"expert": other}, device_id_type=MESH)
+
+    @pl.when(plane < 3)
+    def _():
+        for turn in range(1, early):
+            greet((me + turn) % early)
+
+    @pl.when(plane == 3)
+    def _():
+        for turn in range(1, quarter):
+            greet(early + (place_in + turn) % quarter)
 
     routes_in = pltpu.make_async_copy(routes_ref, named_ref, in_sem.at[pieces])
     routes_in.start()
@@ -80,8 +91,20 @@
 
     middle, last = rows // 2, rows - tok_rows
     send_ref[:middle] = place(0, middle)
-    pl.semaphore_wait(barrier, owners - 1)
-    parity = (me // quarter) % 2
+
+    @pl.when(plane < 3)
+    def _():
+        pl.semaphore_wait(barrier, early - 1)
+        for turn in range(quarter):
+            greet(early + (place_in + turn) % quarter)
+
+    @pl.when(plane == 3)
+    def _():
+        pl.semaphore_wait(barrier, owners - 1)
+        for turn in range(early):
+            greet(turn)
+
+    parity = plane % 2
 
     def exchanged(step, slot):
         return pltpu.make_async_remote_copy(
@@ -97,13 +120,38 @@
         slot = parity * quarter + step % quarter if step < owners // 2 else step
         exchanged(step, slot).start()
 
-    for step in range(owners // 2):
-        send(step)
+    def send_group(group):
+        for step in range(group * quarter, min((group + 1) * quarter, owners - 1)):
+            send(step)
+
+    send_group(0)
+
+    @pl.when(plane >= 2)
+    def _():
+        send_group(1)
+
     rest = place(middle, middle)
     send_ref[middle:] = rest[: last - middle]
     got_ref[last:, :] = rest[last - middle :]
-    for step in range(owners // 2, owners - 1):
-        send(step)
+
+    @pl.when(plane != 2)
+    def _():
+        send_group(2)
+
+    send_group(3)
+
+    @pl.when(plane < 3)
+    def _():
+        pl.semaphore_wait(barrier, quarter)
+
+    @pl.when(plane < 2)
+    def _():
+        send_group(1)
+
+    @pl.when(plane == 2)
+    def _():
+        send_group(2)
+
     for step in range(owners - 1):
         exchanged(step, step).wait()
 

time: 19.2 us -> 18.9 us (0.984)
  Pallas kernels: 19 us -> 18.6 us
    pallas_call x1, Pallas kernels: 16.7 us -> 16.2 us  [exchange(): pl.pallas_call(functools.partial(exchange_kernel, owners), out_shape=jax....]
where the time goes in v4:
time: 18.9 us; the launch traced here: 18.6 us
  Pallas kernels  18.6 us (98%)
    pallas_call x1, Pallas kernels, exchange(): pl.pallas_call(functools.partial(exchange_kernel, owners), out_shape=jax....  16.2 us
    pallas_call x1, Pallas kernels, gram_of(): pl.pallas_call(functools.partial(gram_kernel, scale, tiles), out_shape=ja...  2.35 us

profile of v4, /device:TPU:9, one launch (start us, length us, event | category | flops | bytes accessed | tf_op | source)
XLA Modules:
  0.0 18.6 jit_solution(4587285599744026596)
XLA Ops:
  0.0 16.2 %shard_map.28.rows_ref = bf16[256,1024]{1,0:T(8,128)(2,1)S(1)} custom-call(bf16[128,2,1024]{2,1,0:T(2,128)(2,1)} %bitcast.3, s32[8,16]{1,0:T(8,128)} %bitcast.4), custom_call_target="tpu_custom_call" | custom-call | tf_op jit(solution)/shard_map/pallas_call | solution.py:164
  16.3 2.4 %shard_map.29 = f32[1024,1024]{1,0:T(8,128)} custom-call(bf16[256,1024]{1,0:T(8,128)(2,1)S(1)} %shard_map.28.rows_ref), custom_call_target="tpu_custom_call" | custom-call | tf_op jit(solution)/shard_map/pallas_call | solution.py:203
